TPU v7x, 32 devices: a whole 2x2x4 slice. The times are simulated.
32 devices in a mesh: cells: 8 (over z, y), bands: 4 (over x, core).
Axes of the slice: x: 2, y: 2, z: 4, core: 2. Of those that a mesh axis runs over, the one named last changes fastest.
Arguments:
- psi: bfloat16 [128, 16, 16, 512], P('cells', None, None, 'bands'), may hold values from -64 to 64
- cell_ham: bfloat16 [64, 729, 729], P('cells'), may hold values from -2 to 2
- proj_table: bfloat16 [4, 8, 16, 729], replicated, may hold values from -0.21875 to 0.21875
- coupling: float32 [4, 16, 16], replicated, may hold values from -0.5 to 0.5
- atom_kind: int32 [16, 2, 2], P('cells'), may hold values from -1 to 3, as said below
Outputs:
- filtered: bfloat16 [128, 16, 16, 512], P('cells', None, None, 'bands')
- correlation: float32 [512, 512], P('cells', 'bands')
Inputs may be any that keep to these rules, and one draw needn't show every extreme that they name: `atom_kind`: -1 marks a vertex without an atom; other values name the species.
All inputs are finite; a program needn't handle non-finite values.
Results may differ from a plain program's by a relative error of at most 0.0066.
Values may be sent and summed in bfloat16 or wider, within the bound.
A program may use at most 128 MiB of HBM per device.

v0:
```python
import functools
import jax
import jax.numpy as jnp
from jax import lax
from jax.experimental import pallas as pl
from jax.experimental.pallas import tpu as pltpu
from jax.sharding import PartitionSpec as P

ORDER = 8
CPD = 2
DEGREE = 3
LANES = 128
f32 = jnp.float32
bf16 = jnp.bfloat16

MESSAGES = [(1, 0, 0), (0, 1, 0), (0, 0, 1), (1, 1, 0), (1, 0, 1), (0, 1, 1), (1, 1, 1)]


def cube_root(amount):
    result = 1
    while (result + 1) ** 3 <= amount:
        result = result + 1
    return result


def message_rows(extent, unit):
    starts, start = [], 0
    for m in MESSAGES:
        free = 3 - sum(m)
        rows = max(extent**free * unit, 16)
        starts.append((start, rows))
        start += rows
    return starts, start


def filter_kernel(
    blocks, side, nodes, psi_ref, ham_hbm, table_ref, coupling_ref, kind_ref, out_ref,
    ham, ya, yb, total, vcell, vb, proj, parts, loc, coef, wgt,
    node_out, node_in, vert_out, vert_in,
    node_ssem, node_rsem, vert_ssem, vert_rsem, ham_sem,
):
    block = psi_ref.shape[0]
    edge = block + 1
    pitch = 24
    cells = CPD**3
    cell_edge = ORDER + 1
    kinds = table_ref.shape[0]
    nproj = table_ref.shape[2]
    corners = 8
    corner_span = corners * nproj
    vside = CPD + 1
    me = lax.axis_index("cells")
    offsets = [i * 1 + j * side + k * side * side for i, j, k in MESSAGES]
    ups = [lax.rem(me + o, blocks) for o in offsets]
    downs = [lax.rem(me + blocks - o, blocks) for o in offsets]
    node_rows, _ = message_rows(block, 1)
    vert_rows, _ = message_rows(CPD, nproj)

    ham_copies = [
        pltpu.make_async_copy(ham_hbm.at[c], ham.at[c], ham_sem.at[c]) for c in range(cells)
    ]
    for copy in ham_copies:
        copy.start()

    barrier = pltpu.get_barrier_semaphore()
    for target in ups + downs:
        pl.semaphore_signal(
            barrier, inc=1, device_id={"cells": target}, device_id_type=pl.DeviceIdType.MESH
        )
    pl.semaphore_wait(barrier, len(ups) + len(downs))

    pending = []

    def send(out, arrive, ssem, rsem, ranges, step, targets):
        copies = []
        for m, (start, rows) in enumerate(ranges):
            copy = pltpu.make_async_remote_copy(
                src_ref=out.at[step, pl.ds(start, rows)],
                dst_ref=arrive.at[step, pl.ds(start, rows)],
                send_sem=ssem.at[step, m],
                recv_sem=rsem.at[step, m],
                device_id={"cells": targets[m]},
                device_id_type=pl.DeviceIdType.MESH,
            )
            copy.start()
            copies.append(copy)
        pending.extend(copies)
        return copies

    send_nodes = functools.partial(send, node_out, node_in, node_ssem, node_rsem, node_rows)
    send_verts = functools.partial(send, vert_out, vert_in, vert_ssem, vert_rsem, vert_rows)

    def line(x, y):
        return pl.multiple_of((x * edge + y) * pitch, 8)

    def pack_nodes(field, plane, step):
        (s0, _), (s1, _), (s2, _), (s3, _), (s4, _), (s5, _), (s6, _) = node_rows

        def put(start, value):
            node_out[step, pl.ds(start, block), :] = value.astype(bf16)

        def body(x, carry):
            at = pl.multiple_of(x * block, 16)
            put(s0 + at, field[pl.ds(line(plane, x), block), :])
            put(s1 + at, field[pl.ds(line(x, plane), block), :])
            put(s2 + at, field[pl.ds(line(x, 0) + plane, block, pitch), :])
            return carry

        lax.fori_loop(0, block, body, 0)
        put(s3, field[pl.ds(((plane * edge) + plane) * pitch, block), :])
        put(s4, field[pl.ds((plane * edge) * pitch + plane, block, pitch), :])
        put(s5, field[pl.ds(plane * pitch + plane, block, pitch * edge), :])
        corner = field[pl.ds((plane * edge + plane) * pitch + plane, 1), :]
        put(s6, jnp.broadcast_to(corner, (block, LANES)))

    def unpack_nodes(field, plane, step, add):
        (s0, _), (s1, _), (s2, _), (s3, _), (s4, _), (s5, _), (s6, _) = node_rows

        def put(where, start):
            value = node_in[step, pl.ds(start, block), :].astype(f32)
            if add:
                value = field[where, :] + value
            field[where, :] = value

        def body(x, carry):
            at = pl.multiple_of(x * block, 16)
            put(pl.ds(line(plane, x), block), s0 + at)
            put(pl.ds(line(x, plane), block), s1 + at)
            put(pl.ds(line(x, 0) + plane, block, pitch), s2 + at)
            return carry

        lax.fori_loop(0, block, body, 0)
        put(pl.ds(((plane * edge) + plane) * pitch, block), s3)
        put(pl.ds((plane * edge) * pitch + plane, block, pitch), s4)
        put(pl.ds(plane * pitch + plane, block, pitch * edge), s5)
        where = pl.ds((plane * edge + plane) * pitch + plane, 1)
        value = node_in[step, pl.ds(s6, block), :].astype(f32)[0:1]
        if add:
            value = field[where, :] + value
        field[where, :] = value

    def vertex_places(plane):
        places = []
        for m, (start, _) in zip(MESSAGES, vert_rows):
            spans = [[plane] if fixed else list(range(CPD)) for fixed in m]
            at = start
            for i in spans[0]:
                for j in spans[1]:
                    for k in spans[2]:
                        places.append(((i * vside + j) * vside + k, at))
                        at += nproj
        return places

    def pack_verts(field, plane, step):
        for vertex, at in vertex_places(plane):
            vert_out[step, pl.ds(at, nproj), :] = field[vertex].astype(bf16)

    def unpack_verts(field, plane, step, add):
        for vertex, at in vertex_places(plane):
            value = vert_in[step, pl.ds(at, nproj), :].astype(f32)
            field[vertex] = field[vertex] + value if add else value

    def arrived(copies):
        for copy in copies:
            copy.wait_recv()

    owned = [
        ((i * vside + j) * vside + k, (i * CPD + j) * CPD + k)
        for i in range(CPD) for j in range(CPD) for k in range(CPD)
    ]

    def load_psi(x, carry):
        for y in range(block):
            value = psi_ref[x, y].astype(f32)
            ya[pl.ds(line(x, y), block), :] = value
        return carry

    lax.fori_loop(0, block, load_psi, 0)
    pack_nodes(ya, 0, 0)
    psi_copies = send_nodes(0, downs)
    for vertex, position in owned:
        wgt[vertex] = jnp.full((nproj, LANES), kind_ref[position].astype(f32), f32)
    pack_verts(wgt, 0, 0)
    kind_copies = send_verts(0, downs)

    proj[...] = jnp.zeros_like(proj)
    vcell[...] = jnp.zeros_like(vcell)
    arrived(kind_copies)
    unpack_verts(wgt, CPD, 0, False)

    def place(c):
        ca = c // (CPD * CPD)
        cb = lax.rem(c // CPD, CPD)
        cc = lax.rem(c, CPD)
        return ca, cb, cc

    def corner_vertex(c, o):
        ca, cb, cc = place(c)
        return ((ca + o // 4) * vside + cb + (o // 2) % 2) * vside + cc + o % 2

    def select(c, carry):
        for o in range(corners):
            mark = wgt[corner_vertex(c, o)]
            start = 0
            while start < nodes:
                width = min(LANES, nodes - start)
                chosen = jnp.zeros((nproj, width), f32)
                for q in range(kinds):
                    row = table_ref[q, o, :, start : start + width].astype(f32)
                    chosen = jnp.where(mark[:, :width] == float(q), row, chosen)
                proj[c, o * nproj : (o + 1) * nproj, start : start + width] = chosen.astype(bf16)
                start += LANES
        return carry

    lax.fori_loop(0, cells, select, 0)
    arrived(psi_copies)
    unpack_nodes(ya, block, 0, False)

    def cell_base(c):
        ca, cb, cc = place(c)
        return ((ca * ORDER) * edge + cb * ORDER) * pitch + cc * ORDER

    current, previous = ya, yb
    node_step, vert_step = 1, 1
    for degree in range(DEGREE):

        def gather(c, carry):
            base = cell_base(c)
            for x in range(cell_edge):
                for y in range(cell_edge):
                    at = pl.multiple_of(base + (x * edge + y) * pitch, 8)
                    row = (x * cell_edge + y) * cell_edge
                    vcell[row : row + 8, :] = current[pl.ds(at, 8), :]
                    vcell[row + 8 : row + 9, :] = current[pl.ds(at + 8, 1), :]
            values = vcell[...].astype(bf16)
            vb[c] = values
            parts[c] = jnp.dot(proj[c], values, preferred_element_type=f32)
            return carry

        lax.fori_loop(0, cells, gather, 0)
        coef[...] = jnp.zeros_like(coef)
        for c in range(cells):
            ca, cb, cc = c // 4, (c // 2) % 2, c % 2
            for o in range(corners):
                vertex = ((ca + o // 4) * vside + cb + (o // 2) % 2) * vside + cc + o % 2
                coef[vertex] = coef[vertex] + parts[c, o * nproj : (o + 1) * nproj, :]
        pack_verts(coef, CPD, vert_step)
        coef_copies = send_verts(vert_step, ups)

        if degree == 0:
            for copy in ham_copies:
                copy.wait()

        def multiply(c, carry):
            loc[c, 0:nodes, :] = jnp.dot(ham[c], vb[c, 0:nodes, :], preferred_element_type=f32)
            return carry

        half = cells // 2
        lax.fori_loop(0, half, multiply, 0)
        arrived(coef_copies)
        unpack_verts(coef, 0, vert_step, True)
        for vertex, position in owned:
            kind = kind_ref[position]
            matrix = coupling_ref[jnp.maximum(kind, 0)]
            matrix = jnp.where(kind >= 0, matrix, 0.0)
            value = jnp.dot(
                matrix, coef[vertex], precision=lax.Precision.HIGHEST, preferred_element_type=f32
            )
            wgt[vertex] = value.astype(bf16).astype(f32)
        pack_verts(wgt, 0, vert_step + 1)
        weight_copies = send_verts(vert_step + 1, downs)
        lax.fori_loop(half, cells, multiply, 0)
        total[...] = jnp.zeros_like(total)
        arrived(weight_copies)
        unpack_verts(wgt, CPD, vert_step + 1, False)
        vert_step += 2

        def scatter(c, carry):
            weights = jnp.concatenate([wgt[corner_vertex(c, o)] for o in range(corners)], axis=0)
            term = lax.dot_general(
                proj[c], weights.astype(bf16), (((0,), (0,)), ((), ())), preferred_element_type=f32
            )
            vcell[...] = term
            base = cell_base(c)
            for x in range(cell_edge):
                for y in range(cell_edge):
                    at = pl.multiple_of(base + (x * edge + y) * pitch, 8)
                    row = (x * cell_edge + y) * cell_edge
                    total[pl.ds(at, 8), :] = total[pl.ds(at, 8), :] + (
                        vcell[row : row + 8, :] + loc[c, row : row + 8, :]
                    )
                    total[pl.ds(at + 8, 1), :] = total[pl.ds(at + 8, 1), :] + (
                        vcell[row + 8 : row + 9, :] + loc[c, row + 8 : row + 9, :]
                    )
            return carry

        lax.fori_loop(0, cells, scatter, 0)
        pack_nodes(total, block, node_step)
        fold_copies = send_nodes(node_step, ups)
        arrived(fold_copies)
        unpack_nodes(total, 0, node_step, True)
        node_step += 1
        first, last = degree == 0, degree == DEGREE - 1

        def update(x, carry):
            for y in range(block):
                where = pl.ds(line(x, y), block)
                value = total[where, :] - current[where, :]
                if not first:
                    value = 2.0 * value - previous[where, :]
                value = value.astype(bf16)
                if last:
                    out_ref[x, y] = value
                else:
                    previous[where, :] = value.astype(f32)
            return carry

        lax.fori_loop(0, block, update, 0)
        if not last:
            pack_nodes(previous, 0, node_step)
            field_copies = send_nodes(node_step, downs)
            arrived(field_copies)
            unpack_nodes(previous, block, node_step, False)
            node_step += 1
        current, previous = previous, current

    for copy in pending:
        copy.wait_send()


def run_filter(psi, cell_ham, proj_table, coupling, kinds):
    blocks = lax.axis_size("cells")
    side = cube_root(blocks)
    block = psi.shape[0]
    nodes = cell_ham.shape[-1]
    cells = cell_ham.shape[0]
    padded = -(-nodes // LANES) * LANES
    nproj = proj_table.shape[2]
    corner_span = 8 * nproj
    rows = (block + 1) ** 2 * 24
    node_steps, vert_steps = 2 * DEGREE, 2 * DEGREE + 1
    _, node_buffer = message_rows(block, 1)
    _, vert_buffer = message_rows(CPD, nproj)
    vmem = pl.BlockSpec(memory_space=pltpu.VMEM)
    flops = DEGREE * cells * 2 * LANES * nodes * (nodes + 2 * corner_span)
    return pl.pallas_call(
        functools.partial(filter_kernel, blocks, side, nodes),
        out_shape=jax.ShapeDtypeStruct(psi.shape, bf16),
        in_specs=[
            vmem,
            pl.BlockSpec(memory_space=pl.ANY),
            vmem,
            vmem,
            pl.BlockSpec(memory_space=pltpu.SMEM),
        ],
        out_specs=vmem,
        scratch_shapes=[
            pltpu.VMEM((cells, nodes, nodes), bf16),
            pltpu.VMEM((rows, LANES), f32),
            pltpu.VMEM((rows, LANES), f32),
            pltpu.VMEM((rows, LANES), f32),
            pltpu.VMEM((padded, LANES), f32),
            pltpu.VMEM((cells, padded, LANES), bf16),
            pltpu.VMEM((cells, corner_span, padded), bf16),
            pltpu.VMEM((cells, corner_span, LANES), f32),
            pltpu.VMEM((cells, padded, LANES), f32),
            pltpu.VMEM(((CPD + 1) ** 3, nproj, LANES), f32),
            pltpu.VMEM(((CPD + 1) ** 3, nproj, LANES), f32),
            pltpu.VMEM((node_steps, node_buffer, LANES), bf16),
            pltpu.VMEM((node_steps, node_buffer, LANES), bf16),
            pltpu.VMEM((vert_steps, vert_buffer, LANES), bf16),
            pltpu.VMEM((vert_steps, vert_buffer, LANES), bf16),
            pltpu.SemaphoreType.DMA((node_steps, 7)),
            pltpu.SemaphoreType.DMA((node_steps, 7)),
            pltpu.SemaphoreType.DMA((vert_steps, 7)),
            pltpu.SemaphoreType.DMA((vert_steps, 7)),
            pltpu.SemaphoreType.DMA((cells,)),
        ],
        compiler_params=pltpu.CompilerParams(
            collective_id=0, has_side_effects=True, vmem_limit_bytes=52 * 1024 * 1024
        ),
        cost_estimate=pl.CostEstimate(
            flops=flops, bytes_accessed=cells * nodes * nodes * 2, transcendentals=0
        ),
    )(psi, cell_ham, proj_table, coupling, kinds)


def local(psi, cell_ham, proj_table, coupling, atom_kind):
    blocks = lax.axis_size("cells")
    groups = lax.axis_size("bands")
    band_count = psi.shape[-1]
    filtered = run_filter(psi, cell_ham, proj_table, coupling, atom_kind.reshape(-1))
    flat = filtered.reshape(-1, band_count)
    inverse_count = 1.0 / (flat.shape[0] * blocks)
    share = lax.all_to_all(flat, "bands", 0, 1, tiled=True)
    gram = jnp.einsum("nr,nb->rb", share, share, preferred_element_type=f32) * inverse_count
    bands = band_count * groups
    terms = gram.reshape(blocks, bands // blocks, groups, band_count)
    terms = jnp.transpose(terms, (0, 2, 1, 3)).astype(bf16)
    terms = terms.reshape(blocks * groups, bands // blocks, band_count)
    terms = lax.all_to_all(terms, ("cells", "bands"), 0, 0, tiled=True)
    return (filtered, jnp.sum(terms.astype(f32), axis=0))


def solution(mesh):
    in_specs = (
        P("cells", None, None, "bands"),
        P("cells", None, None),
        P(),
        P(),
        P("cells", None, None),
    )
    out_specs = (P("cells", None, None, "bands"), P("cells", "bands"))
    return jax.shard_map(local, mesh=mesh, in_specs=in_specs, out_specs=out_specs, check_vma=False)
```

profile of v0, /device:TPU:1, one launch (start us, length us, event | category | flops | bytes accessed | tf_op | source)
XLA Modules:
  0.0 146.6 jit_solution(8130098477504874388)
XLA Ops:
  0.6 0.0 copy-start.1
  0.6 0.0 copy-start
  0.7 0.8 reshape.17.kind_ref
  1.5 8.8 %copy.8.ham_hbm = bf16[8,729,729]{2,1,0:T(8,128)(2,1)} copy(bf16[8,729,729]{2,0,1:T(8,128)(2,1)} %param.6) | data formatting | bytes 17006112 | tf_op args[1]
  10.3 0.0 copy-done.1
  10.3 0.0 copy-done
  10.3 87.1 %shard_map.68 = bf16[16,16,16,128]{3,2,1,0:T(8,128)(2,1)S(1)} custom-call(bf16[16,16,16,128]{3,2,1,0:T(8,128)(2,1)} %psi_ref.1, bf16[8,729,729]{2,1,0:T(8,128)(2,1)} %copy.8.ham_hbm, bf16[4,8,16,729]{3,2,1,0:T(8,128)(2,1)S(1)} %copy-done, f32[4,16,16]{2,1,0:T(8,128)S(1)} %copy-done.1, s32[8]{0:T(128)S(1)} %reshape.17.kind_ref), custom_call_target="tpu_custom_call" | custom-call | flops 4411791360 | bytes 8503056 | tf_op jit(solution)/shard_map/pallas_call | solution.py:346
  97.5 0.5 copy.9
  98.0 26.6 %all_to_all.24 = bf16[4,1024,128]{1,2,0:T(8,128)(2,1)S(1)} all-to-all(bf16[4,1024,128]{1,2,0:T(8,128)(2,1)S(1)} %copy.9), channel_id=1, replica_groups=mesh['cells'=8,'bands'=4] {'bands'}, dimensions={0} | all-to-all | bytes 2097152 | tf_op jit(solution)/shard_map/all_to_all | solution.py:395
  124.6 0.7 fusion
  125.4 0.1 convert_element_type.13
  125.5 0.1 copy.10
  125.6 19.3 %all_to_all.25 = bf16[32,64,128]{2,1,0:T(8,128)(2,1)S(1)} all-to-all(bf16[32,64,128]{2,1,0:T(8,128)(2,1)S(1)} %bitcast.10), channel_id=1, replica_groups=mesh['cells'=8,'bands'=4] {'cells','bands'}, dimensions={0} | all-to-all | bytes 1048576 | tf_op jit(solution)/shard_map/all_to_all | solution.py:401
  144.9 0.7 convert_reduce_fusion
  145.6 1.0 copy.12
Async XLA Ops:
  0.6 9.7 %copy-start.1 = (f32[4,16,16]{2,1,0:T(8,128)S(1)}, f32[4,16,16]{2,1,0:T(8,128)}, u32[]{:S(2)}) copy-start(f32[4,16,16]{2,1,0:T(8,128)} %coupling_ref.1) | copy-start | bytes 12292
  0.6 9.7 %copy-start = (bf16[4,8,16,729]{3,2,1,0:T(8,128)(2,1)S(1)}, bf16[4,8,16,729]{3,2,1,0:T(8,128)(2,1)}, u32[]{:S(2)}) copy-start(bf16[4,8,16,729]{3,2,1,0:T(8,128)(2,1)} %table_ref.1) | copy-start | bytes 2239492
where the time goes:
time: 147 us
  Pallas kernels  87.1 us (59%)
  blocking collectives  45.9 us (31%)
  local copies, waits for them, and re-layouts  11.4 us (8%)
    pallas_call x1, Pallas kernels, run_filter(): pl.pallas_call(functools.partial(filter_kernel, blocks, side, nodes), out...  87.1 us
    all_to_all x1, blocking collectives, local(): share = lax.all_to_all(flat, 'bands', 0, 1, tiled=True)  26.6 us
    all_to_all x1, blocking collectives, local(): terms = lax.all_to_all(terms, ('cells', 'bands'), 0, 0, tiled=True)  19.3 us
    unnamed x6, local copies, waits for them, and re-layouts  9.8 us

commit v1 on v0

--- a/solution.py
+++ b/solution.py
@@ -34,10 +34,12 @@
 
 
 def filter_kernel(
-    blocks, side, nodes, psi_ref, ham_hbm, table_ref, coupling_ref, kind_ref, out_ref,
+    blocks, groups, side, nodes, psi_ref, ham_hbm, table_ref, coupling_ref, kind_ref, out_ref, corr_ref,
     ham, ya, yb, total, vcell, vb, proj, parts, loc, coef, wgt,
     node_out, node_in, vert_out, vert_in,
     node_ssem, node_rsem, vert_ssem, vert_rsem, ham_sem,
+    inner, faces, slots, wide, gram_out, gram_in, summed, summed_in,
+    band_ssem, band_rsem, own_sem, cell_ssem, cell_rsem,
 ):
     block = psi_ref.shape[0]
     edge = block + 1
@@ -63,11 +65,18 @@
         copy.start()
 
     barrier = pltpu.get_barrier_semaphore()
-    for target in ups + downs:
+    group = lax.axis_index("bands")
+    cell_peers = [lax.rem(me + j, blocks) for j in range(1, blocks)]
+    band_peers = [lax.rem(group + j, groups) for j in range(1, groups)]
+    for target in cell_peers:
         pl.semaphore_signal(
             barrier, inc=1, device_id={"cells": target}, device_id_type=pl.DeviceIdType.MESH
         )
-    pl.semaphore_wait(barrier, len(ups) + len(downs))
+    for target in band_peers:
+        pl.semaphore_signal(
+            barrier, inc=1, device_id={"bands": target}, device_id_type=pl.DeviceIdType.MESH
+        )
+    pl.semaphore_wait(barrier, len(cell_peers) + len(band_peers))
 
     pending = []
 
@@ -219,6 +228,33 @@
     def cell_base(c):
         ca, cb, cc = place(c)
         return ((ca * ORDER) * edge + cb * ORDER) * pitch + cc * ORDER
+
+    depth = lax.broadcasted_iota(jnp.int32, (block, LANES), 0)
+    share_rows = block**3 // groups
+    face_rows = 3 * block * block // groups
+
+    def share(source, start, rows, kind):
+        copies = []
+        for j, target in enumerate(band_peers):
+            copies.append(
+                pltpu.make_async_remote_copy(
+                    src_ref=source.at[pl.ds(pl.multiple_of(target * rows, 16), rows)],
+                    dst_ref=slots.at[group, pl.ds(start, rows)],
+                    send_sem=band_ssem.at[kind, j],
+                    recv_sem=band_rsem.at[kind, j],
+                    device_id={"bands": target},
+                    device_id_type=pl.DeviceIdType.MESH,
+                )
+            )
+            copies[-1].start()
+        pending.extend(copies)
+        own = pltpu.make_async_copy(
+            source.at[pl.ds(pl.multiple_of(group * rows, 16), rows)],
+            slots.at[group, pl.ds(start, rows)],
+            own_sem.at[kind],
+        )
+        own.start()
+        return copies, own
 
     current, previous = ya, yb
     node_step, vert_step = 1, 1
@@ -283,36 +319,52 @@
             vcell[...] = term
             base = cell_base(c)
             for x in range(cell_edge):
+                stores = []
                 for y in range(cell_edge):
                     at = pl.multiple_of(base + (x * edge + y) * pitch, 8)
                     row = (x * cell_edge + y) * cell_edge
-                    total[pl.ds(at, 8), :] = total[pl.ds(at, 8), :] + (
-                        vcell[row : row + 8, :] + loc[c, row : row + 8, :]
-                    )
-                    total[pl.ds(at + 8, 1), :] = total[pl.ds(at + 8, 1), :] + (
-                        vcell[row + 8 : row + 9, :] + loc[c, row + 8 : row + 9, :]
-                    )
+                    for place_in, rows, size in ((at, row, 8), (at + 8, row + 8, 1)):
+                        where = pl.ds(place_in, size)
+                        value = vcell[rows : rows + size, :] + loc[c, rows : rows + size, :]
+                        stores.append((where, total[where, :] + value))
+                for where, value in stores:
+                    total[where, :] = value
             return carry
 
         lax.fori_loop(0, cells, scatter, 0)
         pack_nodes(total, block, node_step)
         fold_copies = send_nodes(node_step, ups)
+        first, last = degree == 0, degree == DEGREE - 1
+
+        def advanced(x, y):
+            where = pl.ds(line(x, y), block)
+            value = total[where, :] - current[where, :]
+            if not first:
+                value = 2.0 * value - previous[where, :]
+            return value.astype(bf16)
+
+        if last:
+            def interior(x, carry):
+                keep = (depth > 0) & (x > 0)
+                for y in range(1, block):
+                    value = jnp.where(keep, advanced(x, y).astype(f32), 0.0)
+                    inner[pl.ds(pl.multiple_of((x * block + y) * block, 16), block), :] = value.astype(bf16)
+                inner[pl.ds(pl.multiple_of(x * block * block, 16), block), :] = jnp.zeros((block, LANES), bf16)
+                return carry
+
+            lax.fori_loop(0, block, interior, 0)
+            inner_copies = share(inner, 0, share_rows, 0)
         arrived(fold_copies)
         unpack_nodes(total, 0, node_step, True)
         node_step += 1
-        first, last = degree == 0, degree == DEGREE - 1
 
         def update(x, carry):
-            for y in range(block):
-                where = pl.ds(line(x, y), block)
-                value = total[where, :] - current[where, :]
-                if not first:
-                    value = 2.0 * value - previous[where, :]
-                value = value.astype(bf16)
-                if last:
-                    out_ref[x, y] = value
-                else:
-                    previous[where, :] = value.astype(f32)
+            for start in range(0, block, 4):
+                stores = [(y, advanced(x, y)) for y in range(start, start + 4)]
+                for y, value in stores:
+                    if last:
+                        out_ref[x, y] = value
+                    previous[pl.ds(line(x, y), block), :] = value.astype(f32)
             return carry
 
         lax.fori_loop(0, block, update, 0)
@@ -324,13 +376,85 @@
             node_step += 1
         current, previous = previous, current
 
+    lines = block // groups
+
+    def pack_faces(x, carry):
+        at = (x // lines) * face_rows + lax.rem(x, lines) * block
+        rows = lines * block
+        low = current[pl.ds(line(x, 0), block, pitch), :]
+        side_face = jnp.where(depth > 0, current[pl.ds(line(x, 0), block), :], 0.0)
+        front = jnp.where((depth > 0) & (x > 0), current[pl.ds(line(0, x), block), :], 0.0)
+        for part, value in enumerate((low, side_face, front)):
+            faces[pl.ds(pl.multiple_of(at + part * rows, 16), block), :] = value.astype(bf16)
+        return carry
+
+    lax.fori_loop(0, block, pack_faces, 0)
+    face_copies = share(faces, share_rows, face_rows, 1)
+    for copies, own in (inner_copies, face_copies):
+        own.wait()
+        arrived(copies)
+    for g in range(groups):
+        wide[:, g * LANES : (g + 1) * LANES] = slots[g]
+    for g in range(groups):
+        product = lax.dot_general(
+            wide[:, g * LANES : (g + 1) * LANES], wide[...],
+            (((0,), (0,)), ((), ())), preferred_element_type=f32,
+        )
+        for h in range(groups):
+            gram_out[h, g * LANES : (g + 1) * LANES, :] = product[:, h * LANES : (h + 1) * LANES].astype(bf16)
+    gram_copies = []
+    for j, target in enumerate(band_peers):
+        copy = pltpu.make_async_remote_copy(
+            src_ref=gram_out.at[target],
+            dst_ref=gram_in.at[j],
+            send_sem=band_ssem.at[2, j],
+            recv_sem=band_rsem.at[2, j],
+            device_id={"bands": target},
+            device_id_type=pl.DeviceIdType.MESH,
+        )
+        copy.start()
+        gram_copies.append(copy)
+    pending.extend(gram_copies)
+    arrived(gram_copies)
+    share_of = summed.shape[1]
+    scale = 1.0 / (blocks * block**3)
+    tile = max(share_of, 16)
+    for start in range(0, groups * LANES, tile):
+        value = gram_out[group, start : start + tile, :].astype(f32)
+        for j in range(groups - 1):
+            value = value + gram_in[j, start : start + tile, :].astype(f32)
+        value = value * scale
+        for row in range(0, tile, share_of):
+            summed[(start + row) // share_of] = value[row : row + share_of]
+    sum_copies = []
+    for j, target in enumerate(cell_peers):
+        copy = pltpu.make_async_remote_copy(
+            src_ref=summed.at[target],
+            dst_ref=summed_in.at[j],
+            send_sem=cell_ssem.at[j],
+            recv_sem=cell_rsem.at[j],
+            device_id={"cells": target},
+            device_id_type=pl.DeviceIdType.MESH,
+        )
+        copy.start()
+        sum_copies.append(copy)
+    pending.extend(sum_copies)
+    value = summed[me]
+    for j, copy in enumerate(sum_copies):
+        copy.wait_recv()
+        value = value + summed_in[j]
+    corr_ref[...] = value
+
     for copy in pending:
         copy.wait_send()
 
 
 def run_filter(psi, cell_ham, proj_table, coupling, kinds):
     blocks = lax.axis_size("cells")
+    groups = lax.axis_size("bands")
     side = cube_root(blocks)
+    share_of = groups * LANES // blocks
+    slot_rows = (psi.shape[0] ** 3 + 3 * psi.shape[0] ** 2) // groups
     block = psi.shape[0]
     nodes = cell_ham.shape[-1]
     cells = cell_ham.shape[0]
@@ -344,8 +468,11 @@
     vmem = pl.BlockSpec(memory_space=pltpu.VMEM)
     flops = DEGREE * cells * 2 * LANES * nodes * (nodes + 2 * corner_span)
     return pl.pallas_call(
-        functools.partial(filter_kernel, blocks, side, nodes),
-        out_shape=jax.ShapeDtypeStruct(psi.shape, bf16),
+        functools.partial(filter_kernel, blocks, groups, side, nodes),
+        out_shape=(
+            jax.ShapeDtypeStruct(psi.shape, bf16),
+            jax.ShapeDtypeStruct((share_of, LANES), f32),
+        ),
         in_specs=[
             vmem,
             pl.BlockSpec(memory_space=pl.ANY),
@@ -353,7 +480,7 @@
             vmem,
             pl.BlockSpec(memory_space=pltpu.SMEM),
         ],
-        out_specs=vmem,
+        out_specs=(vmem, vmem),
         scratch_shapes=[
             pltpu.VMEM((cells, nodes, nodes), bf16),
             pltpu.VMEM((rows, LANES), f32),
@@ -375,6 +502,19 @@
             pltpu.SemaphoreType.DMA((vert_steps, 7)),
             pltpu.SemaphoreType.DMA((vert_steps, 7)),
             pltpu.SemaphoreType.DMA((cells,)),
+            pltpu.VMEM((block**3, LANES), bf16),
+            pltpu.VMEM((3 * block**2, LANES), bf16),
+            pltpu.VMEM((groups, slot_rows, LANES), bf16),
+            pltpu.VMEM((slot_rows, groups * LANES), bf16),
+            pltpu.VMEM((groups, groups * LANES, LANES), bf16),
+            pltpu.VMEM((groups - 1, groups * LANES, LANES), bf16),
+            pltpu.VMEM((blocks, share_of, LANES), f32),
+            pltpu.VMEM((blocks - 1, share_of, LANES), f32),
+            pltpu.SemaphoreType.DMA((3, groups - 1)),
+            pltpu.SemaphoreType.DMA((3, groups - 1)),
+            pltpu.SemaphoreType.DMA((2,)),
+            pltpu.SemaphoreType.DMA((blocks - 1,)),
+            pltpu.SemaphoreType.DMA((blocks - 1,)),
         ],
         compiler_params=pltpu.CompilerParams(
             collective_id=0, has_side_effects=True, vmem_limit_bytes=52 * 1024 * 1024
@@ -386,20 +526,7 @@
 
 
 def local(psi, cell_ham, proj_table, coupling, atom_kind):
-    blocks = lax.axis_size("cells")
-    groups = lax.axis_size("bands")
-    band_count = psi.shape[-1]
-    filtered = run_filter(psi, cell_ham, proj_table, coupling, atom_kind.reshape(-1))
-    flat = filtered.reshape(-1, band_count)
-    inverse_count = 1.0 / (flat.shape[0] * blocks)
-    share = lax.all_to_all(flat, "bands", 0, 1, tiled=True)
-    gram = jnp.einsum("nr,nb->rb", share, share, preferred_element_type=f32) * inverse_count
-    bands = band_count * groups
-    terms = gram.reshape(blocks, bands // blocks, groups, band_count)
-    terms = jnp.transpose(terms, (0, 2, 1, 3)).astype(bf16)
-    terms = terms.reshape(blocks * groups, bands // blocks, band_count)
-    terms = lax.all_to_all(terms, ("cells", "bands"), 0, 0, tiled=True)
-    return (filtered, jnp.sum(terms.astype(f32), axis=0))
+    return run_filter(psi, cell_ham, proj_table, coupling, atom_kind.reshape(-1))
 
 
 def solution(mesh):

time: 147 us -> 127 us (0.86)
  blocking collectives: 45.9 us -> 0 us
  Pallas kernels: 87.1 us -> 115 us
    all_to_all x2 -> x0, blocking collectives: 45.9 us -> none  [the longest x1 26.6 us: local(): share = lax.all_to_all(flat, 'bands', 0, 1, tiled=True)]
    pallas_call x1, Pallas kernels: 87.1 us -> 115 us  [run_filter(): pl.pallas_call(functools.partial(filter_kernel, blocks, groups, side, nod...]
    unnamed x6 -> x7, local copies, waits for them, and re-layouts: 9.8 us -> 10.4 us
where the time goes in v1:
time: 127 us
  Pallas kernels  115 us (91%)
  local copies, waits for them, and re-layouts  11.3 us (9%)
    pallas_call x1, Pallas kernels, run_filter(): pl.pallas_call(functools.partial(filter_kernel, blocks, groups, side, nod...  115 us
    unnamed x7, local copies, waits for them, and re-layouts  10.4 us

profile of v1, /device:TPU:1, one launch (start us, length us, event | category | flops | bytes accessed | tf_op | source)
XLA Modules:
  0.0 126.6 jit_solution(16752562142590523964)
XLA Ops:
  0.6 0.0 copy-start.1
  0.6 0.0 copy-start
  0.7 0.8 reshape.7.kind_ref
  1.5 8.8 %copy.7.ham_hbm = bf16[8,729,729]{2,1,0:T(8,128)(2,1)} copy(bf16[8,729,729]{2,0,1:T(8,128)(2,1)} %param.6) | data formatting | bytes 17006112 | tf_op args[1]
  10.3 0.0 copy-done.1
  10.3 0.0 copy-done
  10.3 114.7 %shard_map.68 = (bf16[16,16,16,128]{3,2,1,0:T(8,128)(2,1)S(1)}, f32[64,128]{1,0:T(8,128)S(1)}) custom-call(bf16[16,16,16,128]{3,2,1,0:T(8,128)(2,1)} %psi_ref.1, bf16[8,729,729]{2,1,0:T(8,128)(2,1)} %copy.7.ham_hbm, bf16[4,8,16,729]{3,2,1,0:T(8,128)(2,1)S(1)} %copy-done, f32[4,16,16]{2,1,0:T(8,128)S(1)} %copy-done.1, s32[8]{0:T(128)S(1)} %reshape.7.kind_ref), custom_call_target="tpu_custom_call" | custom-call | flops 4411791360 | bytes 8503056 | tf_op jit(solution)/shard_map/pallas_call | solution.py:470
  125.0 1.0 copy.10
  126.0 0.6 copy.11
Async XLA Ops:
  0.6 9.7 %copy-start.1 = (f32[4,16,16]{2,1,0:T(8,128)S(1)}, f32[4,16,16]{2,1,0:T(8,128)}, u32[]{:S(2)}) copy-start(f32[4,16,16]{2,1,0:T(8,128)} %coupling_ref.1) | copy-start | bytes 12292
  0.6 9.7 %copy-start = (bf16[4,8,16,729]{3,2,1,0:T(8,128)(2,1)S(1)}, bf16[4,8,16,729]{3,2,1,0:T(8,128)(2,1)}, u32[]{:S(2)}) copy-start(bf16[4,8,16,729]{3,2,1,0:T(8,128)(2,1)} %table_ref.1) | copy-start | bytes 2239492

commit v2 on v1

--- a/solution.py
+++ b/solution.py
@@ -38,7 +38,7 @@
     ham, ya, yb, total, vcell, vb, proj, parts, loc, coef, wgt,
     node_out, node_in, vert_out, vert_in,
     node_ssem, node_rsem, vert_ssem, vert_rsem, ham_sem,
-    inner, faces, slots, wide, gram_out, gram_in, summed, summed_in,
+    raw, stage, projt, inner, faces, slots, wide, gram_out, gram_in, summed, summed_in,
     band_ssem, band_rsem, own_sem, cell_ssem, cell_rsem,
 ):
     block = psi_ref.shape[0]
@@ -58,11 +58,8 @@
     node_rows, _ = message_rows(block, 1)
     vert_rows, _ = message_rows(CPD, nproj)
 
-    ham_copies = [
-        pltpu.make_async_copy(ham_hbm.at[c], ham.at[c], ham_sem.at[c]) for c in range(cells)
-    ]
-    for copy in ham_copies:
-        copy.start()
+    ham_copy = pltpu.make_async_copy(ham_hbm, raw, ham_sem.at[0])
+    ham_copy.start()
 
     barrier = pltpu.get_barrier_semaphore()
     group = lax.axis_index("bands")
@@ -80,9 +77,10 @@
 
     pending = []
 
-    def send(out, arrive, ssem, rsem, ranges, step, targets):
+    def send(out, arrive, ssem, rsem, ranges, step, targets, chosen=range(7)):
         copies = []
-        for m, (start, rows) in enumerate(ranges):
+        for m in chosen:
+            start, rows = ranges[m]
             copy = pltpu.make_async_remote_copy(
                 src_ref=out.at[step, pl.ds(start, rows)],
                 dst_ref=arrive.at[step, pl.ds(start, rows)],
@@ -102,7 +100,7 @@
     def line(x, y):
         return pl.multiple_of((x * edge + y) * pitch, 8)
 
-    def pack_nodes(field, plane, step):
+    def pack_nodes(field, plane, step, with_x=True, without_x=True):
         (s0, _), (s1, _), (s2, _), (s3, _), (s4, _), (s5, _), (s6, _) = node_rows
 
         def put(start, value):
@@ -110,17 +108,21 @@
 
         def body(x, carry):
             at = pl.multiple_of(x * block, 16)
-            put(s0 + at, field[pl.ds(line(plane, x), block), :])
-            put(s1 + at, field[pl.ds(line(x, plane), block), :])
-            put(s2 + at, field[pl.ds(line(x, 0) + plane, block, pitch), :])
+            if with_x:
+                put(s0 + at, field[pl.ds(line(plane, x), block), :])
+            if without_x:
+                put(s1 + at, field[pl.ds(line(x, plane), block), :])
+                put(s2 + at, field[pl.ds(line(x, 0) + plane, block, pitch), :])
             return carry
 
-        lax.fori_loop(0, block, body, 0)
-        put(s3, field[pl.ds(((plane * edge) + plane) * pitch, block), :])
-        put(s4, field[pl.ds((plane * edge) * pitch + plane, block, pitch), :])
-        put(s5, field[pl.ds(plane * pitch + plane, block, pitch * edge), :])
-        corner = field[pl.ds((plane * edge + plane) * pitch + plane, 1), :]
-        put(s6, jnp.broadcast_to(corner, (block, LANES)))
+        lax.fori_loop(0, block, body, 0, unroll=4)
+        if with_x:
+            put(s3, field[pl.ds(((plane * edge) + plane) * pitch, block), :])
+            put(s4, field[pl.ds((plane * edge) * pitch + plane, block, pitch), :])
+            corner = field[pl.ds((plane * edge + plane) * pitch + plane, 1), :]
+            put(s6, jnp.broadcast_to(corner, (block, LANES)))
+        if without_x:
+            put(s5, field[pl.ds(plane * pitch + plane, block, pitch * edge), :])
 
     def unpack_nodes(field, plane, step, add):
         (s0, _), (s1, _), (s2, _), (s3, _), (s4, _), (s5, _), (s6, _) = node_rows
@@ -192,6 +194,27 @@
     pack_verts(wgt, 0, 0)
     kind_copies = send_verts(0, downs)
 
+    full, tail = nodes // 16, nodes % 16
+    chunks = [(n, start, min(LANES, nodes - start)) for n, start in enumerate(range(0, nodes, LANES))]
+
+    def relayout(t, rows):
+        for r in range(rows):
+            value = raw[t * 16 + r].astype(f32)
+            for n, start, width in chunks:
+                stage[n, r * cells : (r + 1) * cells, 0:width] = value[:, start : start + width]
+        for c in range(cells):
+            for n, start, _ in chunks:
+                value = stage[n, pl.ds(c, 16, cells), :].astype(bf16)
+                ham[c, pl.ds(pl.multiple_of(t * 16, 16), 16), start : start + LANES] = value
+
+    def relayout_body(t, carry):
+        relayout(t, 16)
+        return carry
+
+    early = full * 2 // 3
+    stage[...] = jnp.zeros_like(stage)
+    ham_copy.wait()
+    lax.fori_loop(0, early, relayout_body, 0)
     proj[...] = jnp.zeros_like(proj)
     vcell[...] = jnp.zeros_like(vcell)
     arrived(kind_copies)
@@ -219,6 +242,7 @@
                     chosen = jnp.where(mark[:, :width] == float(q), row, chosen)
                 proj[c, o * nproj : (o + 1) * nproj, start : start + width] = chosen.astype(bf16)
                 start += LANES
+        projt[c] = jnp.transpose(proj[c].astype(f32)).astype(bf16)
         return carry
 
     lax.fori_loop(0, cells, select, 0)
@@ -273,7 +297,7 @@
             parts[c] = jnp.dot(proj[c], values, preferred_element_type=f32)
             return carry
 
-        lax.fori_loop(0, cells, gather, 0)
+        lax.fori_loop(0, cells, gather, 0, unroll=2)
         coef[...] = jnp.zeros_like(coef)
         for c in range(cells):
             ca, cb, cc = c // 4, (c // 2) % 2, c % 2
@@ -284,11 +308,13 @@
         coef_copies = send_verts(vert_step, ups)
 
         if degree == 0:
-            for copy in ham_copies:
-                copy.wait()
+            lax.fori_loop(early, full, relayout_body, 0)
+            if tail:
+                stage[:, tail * cells :, :] = jnp.zeros((len(chunks), (16 - tail) * cells, LANES), f32)
+                relayout(full, tail)
 
         def multiply(c, carry):
-            loc[c, 0:nodes, :] = jnp.dot(ham[c], vb[c, 0:nodes, :], preferred_element_type=f32)
+            loc[c, 0 : ham.shape[1], :] = jnp.dot(ham[c], vb[c], preferred_element_type=f32)
             return carry
 
         half = cells // 2
@@ -313,10 +339,7 @@
 
         def scatter(c, carry):
             weights = jnp.concatenate([wgt[corner_vertex(c, o)] for o in range(corners)], axis=0)
-            term = lax.dot_general(
-                proj[c], weights.astype(bf16), (((0,), (0,)), ((), ())), preferred_element_type=f32
-            )
-            vcell[...] = term
+            vcell[...] = jnp.dot(projt[c], weights.astype(bf16), preferred_element_type=f32)
             base = cell_base(c)
             for x in range(cell_edge):
                 stores = []
@@ -331,9 +354,12 @@
                     total[where, :] = value
             return carry
 
-        lax.fori_loop(0, cells, scatter, 0)
-        pack_nodes(total, block, node_step)
-        fold_copies = send_nodes(node_step, ups)
+        lax.fori_loop(half, cells, scatter, 0)
+        pack_nodes(total, block, node_step, without_x=False)
+        fold_copies = send_nodes(node_step, ups, [m for m in range(7) if MESSAGES[m][0]])
+        lax.fori_loop(0, half, scatter, 0)
+        pack_nodes(total, block, node_step, with_x=False)
+        fold_copies += send_nodes(node_step, ups, [m for m in range(7) if not MESSAGES[m][0]])
         first, last = degree == 0, degree == DEGREE - 1
 
         def advanced(x, y):
@@ -425,7 +451,7 @@
             value = value + gram_in[j, start : start + tile, :].astype(f32)
         value = value * scale
         for row in range(0, tile, share_of):
-            summed[(start + row) // share_of] = value[row : row + share_of]
+            summed[(start + row) // share_of] = value[row : row + share_of].astype(summed.dtype)
     sum_copies = []
     for j, target in enumerate(cell_peers):
         copy = pltpu.make_async_remote_copy(
@@ -439,10 +465,10 @@
         copy.start()
         sum_copies.append(copy)
     pending.extend(sum_copies)
-    value = summed[me]
+    value = summed[me].astype(f32)
     for j, copy in enumerate(sum_copies):
         copy.wait_recv()
-        value = value + summed_in[j]
+        value = value + summed_in[j].astype(f32)
     corr_ref[...] = value
 
     for copy in pending:
@@ -454,6 +480,7 @@
     groups = lax.axis_size("bands")
     side = cube_root(blocks)
     share_of = groups * LANES // blocks
+    sum_type = f32 if share_of % 16 else bf16
     slot_rows = (psi.shape[0] ** 3 + 3 * psi.shape[0] ** 2) // groups
     block = psi.shape[0]
     nodes = cell_ham.shape[-1]
@@ -482,7 +509,7 @@
         ],
         out_specs=(vmem, vmem),
         scratch_shapes=[
-            pltpu.VMEM((cells, nodes, nodes), bf16),
+            pltpu.VMEM((cells, -(-nodes // 16) * 16, padded), bf16),
             pltpu.VMEM((rows, LANES), f32),
             pltpu.VMEM((rows, LANES), f32),
             pltpu.VMEM((rows, LANES), f32),
@@ -501,15 +528,18 @@
             pltpu.SemaphoreType.DMA((node_steps, 7)),
             pltpu.SemaphoreType.DMA((vert_steps, 7)),
             pltpu.SemaphoreType.DMA((vert_steps, 7)),
-            pltpu.SemaphoreType.DMA((cells,)),
+            pltpu.SemaphoreType.DMA((1,)),
+            pltpu.VMEM((nodes, cells, nodes), bf16),
+            pltpu.VMEM((padded // LANES, 16 * cells, LANES), f32),
+            pltpu.VMEM((cells, padded, corner_span), bf16),
             pltpu.VMEM((block**3, LANES), bf16),
             pltpu.VMEM((3 * block**2, LANES), bf16),
             pltpu.VMEM((groups, slot_rows, LANES), bf16),
             pltpu.VMEM((slot_rows, groups * LANES), bf16),
             pltpu.VMEM((groups, groups * LANES, LANES), bf16),
             pltpu.VMEM((groups - 1, groups * LANES, LANES), bf16),
-            pltpu.VMEM((blocks, share_of, LANES), f32),
-            pltpu.VMEM((blocks - 1, share_of, LANES), f32),
+            pltpu.VMEM((blocks, share_of, LANES), sum_type),
+            pltpu.VMEM((blocks - 1, share_of, LANES), sum_type),
             pltpu.SemaphoreType.DMA((3, groups - 1)),
             pltpu.SemaphoreType.DMA((3, groups - 1)),
             pltpu.SemaphoreType.DMA((2,)),
@@ -517,12 +547,12 @@
             pltpu.SemaphoreType.DMA((blocks - 1,)),
         ],
         compiler_params=pltpu.CompilerParams(
-            collective_id=0, has_side_effects=True, vmem_limit_bytes=52 * 1024 * 1024
+            collective_id=0, has_side_effects=True, vmem_limit_bytes=58 * 1024 * 1024
         ),
         cost_estimate=pl.CostEstimate(
             flops=flops, bytes_accessed=cells * nodes * nodes * 2, transcendentals=0
         ),
-    )(psi, cell_ham, proj_table, coupling, kinds)
+    )(psi, jnp.transpose(cell_ham, (1, 0, 2)), proj_table, coupling, kinds)
 
 
 def local(psi, cell_ham, proj_table, coupling, atom_kind):

time: 127 us -> 117 us (0.921)
  local copies, waits for them, and re-layouts: 11.3 us -> 5.07 us
  Pallas kernels: 115 us -> 111 us
    unnamed x7 -> x2, local copies, waits for them, and re-layouts: 10.4 us -> 3.8 us
    pallas_call x1, Pallas kernels: 115 us -> 111 us  [run_filter(): pl.pallas_call(functools.partial(filter_kernel, blocks, groups, side, nod...]
where the time goes in v2:
time: 117 us
  Pallas kernels  111 us (95%)
  local copies, waits for them, and re-layouts  5.07 us (4%)
    pallas_call x1, Pallas kernels, run_filter(): pl.pallas_call(functools.partial(filter_kernel, blocks, groups, side, nod...  111 us
    unnamed x2, local copies, waits for them, and re-layouts  3.8 us

profile of v2, /device:TPU:1, one launch (start us, length us, event | category | flops | bytes accessed | tf_op | source)
XLA Modules:
  0.0 117.2 jit_solution(7217234058540578741)
XLA Ops:
  0.6 1.3 %reshape.7.kind_ref = s32[8]{0:T(128)} reshape(s32[2,2,2]{2,1,0:T(2,128)} %param.9) | data formatting | bytes 64 | tf_op jit(solution)/shard_map/reshape | solution.py:559
  1.9 111.5 %shard_map.68 = (bf16[16,16,16,128]{3,2,1,0:T(8,128)(2,1)}, f32[64,128]{1,0:T(8,128)}) custom-call(bf16[16,16,16,128]{3,2,1,0:T(8,128)(2,1)} %psi_ref.1, bf16[729,8,729]{2,1,0:T(8,128)(2,1)} %bitcast.1, bf16[4,8,16,729]{3,2,1,0:T(8,128)(2,1)} %table_ref.1, f32[4,16,16]{2,1,0:T(8,128)} %coupling_ref.1, s32[8]{0:T(128)} %reshape.7.kind_ref), custom_call_target="tpu_custom_call" | custom-call | flops 4411791360 | bytes 8503056 | tf_op jit(solution)/shard_map/pallas_call | solution.py:497
  113.4 2.4 %copy.9 = bf16[16,16,16,128]{3,2,1,0:T(8,128)(2,1)} copy(bf16[16,16,16,128]{3,2,1,0:T(8,128)(2,1)} %get-tuple-element.4) | data formatting | bytes 2097152
  115.8 1.4 %copy.10 = f32[64,128]{1,0:T(8,128)} copy(f32[64,128]{1,0:T(8,128)} %get-tuple-element.5) | data formatting | bytes 65536

commit v3 on v2

--- a/solution.py
+++ b/solution.py
@@ -100,7 +100,7 @@
     def line(x, y):
         return pl.multiple_of((x * edge + y) * pitch, 8)
 
-    def pack_nodes(field, plane, step, with_x=True, without_x=True):
+    def pack_nodes(field, plane, step, part):
         (s0, _), (s1, _), (s2, _), (s3, _), (s4, _), (s5, _), (s6, _) = node_rows
 
         def put(start, value):
@@ -108,21 +108,30 @@
 
         def body(x, carry):
             at = pl.multiple_of(x * block, 16)
-            if with_x:
+            if part == 0:
                 put(s0 + at, field[pl.ds(line(plane, x), block), :])
-            if without_x:
+            elif part == 1:
                 put(s1 + at, field[pl.ds(line(x, plane), block), :])
+            else:
                 put(s2 + at, field[pl.ds(line(x, 0) + plane, block, pitch), :])
             return carry
 
         lax.fori_loop(0, block, body, 0, unroll=4)
-        if with_x:
+        if part == 1:
             put(s3, field[pl.ds(((plane * edge) + plane) * pitch, block), :])
+        elif part == 2:
             put(s4, field[pl.ds((plane * edge) * pitch + plane, block, pitch), :])
+            put(s5, field[pl.ds(plane * pitch + plane, block, pitch * edge), :])
             corner = field[pl.ds((plane * edge + plane) * pitch + plane, 1), :]
             put(s6, jnp.broadcast_to(corner, (block, LANES)))
-        if without_x:
-            put(s5, field[pl.ds(plane * pitch + plane, block, pitch * edge), :])
+
+    def ship_nodes(field, plane, step, targets, parts=(2, 1, 0)):
+        copies = []
+        for part in parts:
+            pack_nodes(field, plane, step, part)
+            chosen = [m for m in range(7) if max(d for d in range(3) if MESSAGES[m][d]) == part]
+            copies += send_nodes(step, targets, chosen)
+        return copies
 
     def unpack_nodes(field, plane, step, add):
         (s0, _), (s1, _), (s2, _), (s3, _), (s4, _), (s5, _), (s6, _) = node_rows
@@ -187,10 +196,9 @@
         return carry
 
     lax.fori_loop(0, block, load_psi, 0)
-    pack_nodes(ya, 0, 0)
-    psi_copies = send_nodes(0, downs)
+    psi_copies = ship_nodes(ya, 0, 0, downs)
     for vertex, position in owned:
-        wgt[vertex] = jnp.full((nproj, LANES), kind_ref[position].astype(f32), f32)
+        wgt[vertex] = jnp.full((nproj, LANES), kind_ref[position // 4, (position // 2) % 2, position % 2].astype(f32), f32)
     pack_verts(wgt, 0, 0)
     kind_copies = send_verts(0, downs)
 
@@ -322,7 +330,7 @@
         arrived(coef_copies)
         unpack_verts(coef, 0, vert_step, True)
         for vertex, position in owned:
-            kind = kind_ref[position]
+            kind = kind_ref[position // 4, (position // 2) % 2, position % 2]
             matrix = coupling_ref[jnp.maximum(kind, 0)]
             matrix = jnp.where(kind >= 0, matrix, 0.0)
             value = jnp.dot(
@@ -354,12 +362,13 @@
                     total[where, :] = value
             return carry
 
-        lax.fori_loop(half, cells, scatter, 0)
-        pack_nodes(total, block, node_step, without_x=False)
-        fold_copies = send_nodes(node_step, ups, [m for m in range(7) if MESSAGES[m][0]])
-        lax.fori_loop(0, half, scatter, 0)
-        pack_nodes(total, block, node_step, with_x=False)
-        fold_copies += send_nodes(node_step, ups, [m for m in range(7) if not MESSAGES[m][0]])
+        fold_copies = []
+        for part, stride in ((2, 2), (1, CPD * CPD), (0, CPD * CPD)):
+            start = (0, 2, 1)[part]
+            lax.fori_loop(
+                0, cells // stride, lambda t, carry: scatter(t * stride + start, carry), 0
+            )
+            fold_copies += ship_nodes(total, block, node_step, ups, (part,))
         first, last = degree == 0, degree == DEGREE - 1
 
         def advanced(x, y):
@@ -395,8 +404,7 @@
 
         lax.fori_loop(0, block, update, 0)
         if not last:
-            pack_nodes(previous, 0, node_step)
-            field_copies = send_nodes(node_step, downs)
+            field_copies = ship_nodes(previous, 0, node_step, downs)
             arrived(field_copies)
             unpack_nodes(previous, block, node_step, False)
             node_step += 1
@@ -547,7 +555,7 @@
             pltpu.SemaphoreType.DMA((blocks - 1,)),
         ],
         compiler_params=pltpu.CompilerParams(
-            collective_id=0, has_side_effects=True, vmem_limit_bytes=58 * 1024 * 1024
+            collective_id=0, has_side_effects=True, vmem_limit_bytes=50 * 1024 * 1024
         ),
         cost_estimate=pl.CostEstimate(
             flops=flops, bytes_accessed=cells * nodes * nodes * 2, transcendentals=0
@@ -556,7 +564,7 @@
 
 
 def local(psi, cell_ham, proj_table, coupling, atom_kind):
-    return run_filter(psi, cell_ham, proj_table, coupling, atom_kind.reshape(-1))
+    return run_filter(psi, cell_ham, proj_table, coupling, atom_kind)
 
 
 def solution(mesh):

time: 117 us -> 113 us (0.966)
  Pallas kernels: 111 us -> 106 us
    pallas_call x1, Pallas kernels: 111 us -> 106 us  [run_filter(): pl.pallas_call(functools.partial(filter_kernel, blocks, groups, side, nod...]
    unnamed x2 -> x10, local copies, waits for them, and re-layouts: 3.8 us -> 5.38 us
    reshape x1 -> x0, local copies, waits for them, and re-layouts: 1.27 us -> none  [local(): atom_kind.reshape(-1)]
where the time goes in v3:
time: 113 us; the launch traced here: 112 us
  Pallas kernels  106 us (94%)
  local copies, waits for them, and re-layouts  5.38 us (5%)
    pallas_call x1, Pallas kernels, run_filter(): pl.pallas_call(functools.partial(filter_kernel, blocks, groups, side, nod...  106 us
    unnamed x10, local copies, waits for them, and re-layouts  5.38 us

profile of v3, /device:TPU:1, one launch (start us, length us, event | category | flops | bytes accessed | tf_op | source)
XLA Modules:
  0.0 112.4 jit_solution(15379285821500996843)
XLA Ops:
  0.6 0.0 copy-start
  0.6 1.2 %copy-done = bf16[16,16,16,128]{3,2,1,0:T(8,128)(2,1)S(1)} copy-done((bf16[16,16,16,128]{3,2,1,0:T(8,128)(2,1)S(1)}, bf16[16,16,16,128]{3,2,1,0:T(8,128)(2,1)}, u32[]{:S(2)}) %copy-start) | copy-done | bytes 1048600
  1.9 0.0 copy-start.1
  1.9 1.1 %copy-done.1 = bf16[4,8,16,729]{3,2,1,0:T(8,128)(2,1)S(1)} copy-done((bf16[4,8,16,729]{3,2,1,0:T(8,128)(2,1)S(1)}, bf16[4,8,16,729]{3,2,1,0:T(8,128)(2,1)}, u32[]{:S(2)}) %copy-start.1) | copy-done | bytes 746520
  3.0 0.0 copy-start.2
  3.0 0.8 copy-done.2
  3.7 0.0 copy-start.3
  3.8 0.7 copy-done.3
  4.4 106.3 %shard_map.68 = (bf16[16,16,16,128]{3,2,1,0:T(8,128)(2,1)S(1)}, f32[64,128]{1,0:T(8,128)S(1)}) custom-call(bf16[16,16,16,128]{3,2,1,0:T(8,128)(2,1)S(1)} %copy-done, bf16[729,8,729]{2,1,0:T(8,128)(2,1)} %bitcast.1, bf16[4,8,16,729]{3,2,1,0:T(8,128)(2,1)S(1)} %copy-done.1, f32[4,16,16]{2,1,0:T(8,128)S(1)} %copy-done.2, s32[2,2,2]{2,1,0:T(2,128)S(1)} %copy-done.3), custom_call_target="tpu_custom_call" | custom-call | flops 4411791360 | bytes 8503056 | tf_op jit(solution)/shard_map/pallas_call | solution.py:505
  110.8 1.0 copy.9
  111.8 0.6 copy.10
Async XLA Ops:
  0.6 1.2 %copy-start = (bf16[16,16,16,128]{3,2,1,0:T(8,128)(2,1)S(1)}, bf16[16,16,16,128]{3,2,1,0:T(8,128)(2,1)}, u32[]{:S(2)}) copy-start(bf16[16,16,16,128]{3,2,1,0:T(8,128)(2,1)} %psi_ref.1) | copy-start | bytes 3145732
  1.9 1.1 %copy-start.1 = (bf16[4,8,16,729]{3,2,1,0:T(8,128)(2,1)S(1)}, bf16[4,8,16,729]{3,2,1,0:T(8,128)(2,1)}, u32[]{:S(2)}) copy-start(bf16[4,8,16,729]{3,2,1,0:T(8,128)(2,1)} %table_ref.1) | copy-start | bytes 2239492
  3.0 0.8 copy-start.2
  3.7 0.7 copy-start.3

commit v4 on v3

--- a/solution.py
+++ b/solution.py
@@ -149,7 +149,7 @@
             put(pl.ds(line(x, 0) + plane, block, pitch), s2 + at)
             return carry
 
-        lax.fori_loop(0, block, body, 0)
+        lax.fori_loop(0, block, body, 0, unroll=4)
         put(pl.ds(((plane * edge) + plane) * pitch, block), s3)
         put(pl.ds((plane * edge) * pitch + plane, block, pitch), s4)
         put(pl.ds(plane * pitch + plane, block, pitch * edge), s5)
@@ -326,7 +326,7 @@
             return carry
 
         half = cells // 2
-        lax.fori_loop(0, half, multiply, 0)
+        lax.fori_loop(0, half, multiply, 0, unroll=2)
         arrived(coef_copies)
         unpack_verts(coef, 0, vert_step, True)
         for vertex, position in owned:
@@ -339,7 +339,7 @@
             wgt[vertex] = value.astype(bf16).astype(f32)
         pack_verts(wgt, 0, vert_step + 1)
         weight_copies = send_verts(vert_step + 1, downs)
-        lax.fori_loop(half, cells, multiply, 0)
+        lax.fori_loop(half, cells, multiply, 0, unroll=2)
         total[...] = jnp.zeros_like(total)
         arrived(weight_copies)
         unpack_verts(wgt, CPD, vert_step + 1, False)

time: 113 us -> 113 us (level)
  no operation moved by 1% of the time
where the time goes in v4:
time: 113 us; the launch traced here: 112 us
  Pallas kernels  106 us (94%)
  local copies, waits for them, and re-layouts  5.38 us (5%)
    pallas_call x1, Pallas kernels, run_filter(): pl.pallas_call(functools.partial(filter_kernel, blocks, groups, side, nod...  106 us
    unnamed x10, local copies, waits for them, and re-layouts  5.38 us

profile of v4, /device:TPU:1, one launch (start us, length us, event | category | flops | bytes accessed | tf_op | source)
XLA Modules:
  0.0 112.2 jit_solution(5247580316454624034)
XLA Ops:
  0.6 0.0 copy-start
  0.6 1.2 %copy-done = bf16[16,16,16,128]{3,2,1,0:T(8,128)(2,1)S(1)} copy-done((bf16[16,16,16,128]{3,2,1,0:T(8,128)(2,1)S(1)}, bf16[16,16,16,128]{3,2,1,0:T(8,128)(2,1)}, u32[]{:S(2)}) %copy-start) | copy-done | bytes 1048600
  1.9 0.0 copy-start.1
  1.9 1.1 %copy-done.1 = bf16[4,8,16,729]{3,2,1,0:T(8,128)(2,1)S(1)} copy-done((bf16[4,8,16,729]{3,2,1,0:T(8,128)(2,1)S(1)}, bf16[4,8,16,729]{3,2,1,0:T(8,128)(2,1)}, u32[]{:S(2)}) %copy-start.1) | copy-done | bytes 746520
  3.0 0.0 copy-start.2
  3.0 0.8 copy-done.2
  3.7 0.0 copy-start.3
  3.8 0.7 copy-done.3
  4.4 106.2 %shard_map.68 = (bf16[16,16,16,128]{3,2,1,0:T(8,128)(2,1)S(1)}, f32[64,128]{1,0:T(8,128)S(1)}) custom-call(bf16[16,16,16,128]{3,2,1,0:T(8,128)(2,1)S(1)} %copy-done, bf16[729,8,729]{2,1,0:T(8,128)(2,1)} %bitcast.1, bf16[4,8,16,729]{3,2,1,0:T(8,128)(2,1)S(1)} %copy-done.1, f32[4,16,16]{2,1,0:T(8,128)S(1)} %copy-done.2, s32[2,2,2]{2,1,0:T(2,128)S(1)} %copy-done.3), custom_call_target="tpu_custom_call" | custom-call | flops 4411791360 | bytes 8503056 | tf_op jit(solution)/shard_map/pallas_call | solution.py:505
  110.6 1.0 copy.9
  111.6 0.6 copy.10
Async XLA Ops:
  0.6 1.2 %copy-start = (bf16[16,16,16,128]{3,2,1,0:T(8,128)(2,1)S(1)}, bf16[16,16,16,128]{3,2,1,0:T(8,128)(2,1)}, u32[]{:S(2)}) copy-start(bf16[16,16,16,128]{3,2,1,0:T(8,128)(2,1)} %psi_ref.1) | copy-start | bytes 3145732
  1.9 1.1 %copy-start.1 = (bf16[4,8,16,729]{3,2,1,0:T(8,128)(2,1)S(1)}, bf16[4,8,16,729]{3,2,1,0:T(8,128)(2,1)}, u32[]{:S(2)}) copy-start(bf16[4,8,16,729]{3,2,1,0:T(8,128)(2,1)} %table_ref.1) | copy-start | bytes 2239492
  3.0 0.8 copy-start.2
  3.7 0.7 copy-start.3
